TPU v7x, 32 devices: a whole 2x2x4 slice. The times are simulated.
32 devices in a mesh: planes: 8 (over y, x, core), rows: 4 (over z).
Axes of the slice: x: 2, y: 2, z: 4, core: 2. Of those that a mesh axis runs over, the one named last changes fastest.
Arguments:
- observed: float32 [8, 1024, 1024], P('planes', 'rows'), may hold values from -6 to 6
- estimate: float32 [8, 1024, 1024], P('planes', 'rows'), may hold values from -6 to 6
- spectrum: float32 [8, 1024, 1024], P('planes', 'rows'), may hold values from 0.1 to 1
Outputs:
- restored: float32 [8, 1024, 1024], P('planes', 'rows')
- residual: float32 [8, 1024, 1024], P('planes', 'rows')
All inputs are finite; a program needn't handle non-finite values.
Results may differ from a plain program's by a relative error of at most 0.00014.
Values sent between devices are 32-bit elements; how exact they have to be, the bound alone decides.
A program may use at most 128 MiB of HBM per device.

v0:
```python
import functools
import math

import jax
import jax.numpy as jnp
import numpy as np
from jax import lax
from jax.experimental import pallas as pl
from jax.experimental.pallas import tpu as pltpu
from jax.sharding import PartitionSpec as P

HUBER_EDGE = 0.5
SMOOTHING = 0.3
MESH = pl.DeviceIdType.MESH
F32 = jnp.float32
BF16 = jnp.bfloat16
STRIP = 8
VMEM_LIMIT = 56 * 1024 * 1024


def cosine_parts(extent):
    frequency = np.arange(extent)[:, None]
    sample = np.arange(extent)[None, :]
    angles = ((2 * sample + 1) * frequency % (4 * extent)) * (math.pi / (2.0 * extent))
    norming = np.where(frequency == 0, math.sqrt(1.0 / extent), math.sqrt(2.0 / extent))
    whole = (np.cos(angles) * norming).astype(np.float32)
    high = whole.astype(jnp.bfloat16)
    low = (whole - high.astype(np.float32)).astype(jnp.bfloat16)
    return high, low


def halves(x):
    high = x.astype(BF16)
    return high, (x - high.astype(F32)).astype(BF16)


def product(ah, al, bh, bl):
    dot = functools.partial(jnp.dot, preferred_element_type=F32)
    return dot(ah, bh) + (dot(ah, bl) + dot(al, bh))


def folded(x):
    return jnp.sum(x.reshape(x.shape[0] // 8, 8, x.shape[1]), axis=0)


def kernel(
    planes, rows,
    obs, est, spec, c_hi, c_lo, t_hi, t_lo,
    d_out, image, step_out,
    v, pp, pm, w, w_pm, smooth, d, d_pp, d_pm,
    sent, got, back_sent, back_got, seen, xh, xl, yh, yl,
    acc_rr, acc_dot, part, total, red_rows, red_planes,
    send_sem, recv_sem, halo_send, halo_recv, sum_send, sum_recv, sum2_send, sum2_recv,
):
    p, z = lax.axis_index("planes"), lax.axis_index("rows")
    R, N = est.shape
    L = N // rows
    tile = min(256, N)
    my_row = pl.multiple_of(z * R, R)
    my_col = pl.multiple_of(z * L, L)
    has_pm, has_pp = p > 0, p < planes - 1
    has_up, has_dn = z > 0, z < rows - 1

    v[pl.ds(8, R), :] = est[...]

    barrier = pltpu.get_barrier_semaphore()

    def greet(cond, where):
        @pl.when(cond)
        def _():
            pl.semaphore_signal(barrier, inc=1, device_id=where, device_id_type=MESH)

    for o in range(1, rows):
        pl.semaphore_signal(
            barrier, inc=1, device_id=(p, lax.rem(z + o, rows)), device_id_type=MESH
        )
    for o in range(1, planes):
        pl.semaphore_signal(
            barrier, inc=1, device_id=(lax.rem(p + o, planes), z), device_id_type=MESH
        )
    diagonals = (
        (jnp.logical_and(has_pm, has_dn), (p - 1, z + 1)),
        (jnp.logical_and(has_pp, has_up), (p + 1, z - 1)),
    )
    for cond, where in diagonals:
        greet(cond, where)
    peers = rows - 1 + planes - 1
    for cond, _ in diagonals:
        peers = peers + jnp.where(cond, 1, 0)
    pl.semaphore_wait(barrier, peers)

    def forward_copy(kind, o):
        to = lax.rem(z + o, rows)
        src = spec if kind == 0 else sent.at[kind - 1]
        return pltpu.make_async_remote_copy(
            src_ref=src.at[:, pl.ds(pl.multiple_of(to * L, L), L)],
            dst_ref=got.at[kind, pl.ds(my_row, R), :],
            send_sem=send_sem.at[kind, o],
            recv_sem=recv_sem.at[kind, o],
            device_id=(p, to),
            device_id_type=MESH,
        )

    def back_copy(kind, o):
        to = lax.rem(z + o, rows)
        return pltpu.make_async_remote_copy(
            src_ref=back_sent.at[kind, pl.ds(pl.multiple_of(to * R, R), R), :],
            dst_ref=back_got.at[kind, :, pl.ds(my_col, L)],
            send_sem=send_sem.at[kind + 4, o],
            recv_sem=recv_sem.at[kind + 4, o],
            device_id=(p, to),
            device_id_type=MESH,
        )

    first, last = pl.ds(0, 8), pl.ds(R - 8, 8)
    body = pl.ds(8, R)
    both = jnp.logical_and
    links = [
        (est, pm.at[body, :], (p + 1, z), has_pp, has_pm),
        (est, pp.at[body, :], (p - 1, z), has_pm, has_pp),
        (est.at[last, :], v.at[pl.ds(0, 8), :], (p, z + 1), has_dn, has_up),
        (est.at[first, :], v.at[pl.ds(R + 8, 8), :], (p, z - 1), has_up, has_dn),
        (est.at[last, :], pp.at[pl.ds(0, 8), :], (p - 1, z + 1), both(has_pm, has_dn), both(has_pp, has_up)),
        (est.at[first, :], pm.at[pl.ds(R + 8, 8), :], (p + 1, z - 1), both(has_pp, has_up), both(has_pm, has_dn)),
        (d.at[body, :], d_pm, (p + 1, z), has_pp, has_pm),
        (d.at[body, :], d_pp, (p - 1, z), has_pm, has_pp),
        (d.at[pl.ds(R, 8), :], d.at[pl.ds(0, 8), :], (p, z + 1), has_dn, has_up),
        (d.at[pl.ds(8, 8), :], d.at[pl.ds(R + 8, 8), :], (p, z - 1), has_up, has_dn),
    ]

    def link(i, act):
        src, dst, where, sends, receives = links[i]
        copy = pltpu.make_async_remote_copy(
            src_ref=src, dst_ref=dst, send_sem=halo_send.at[i], recv_sem=halo_recv.at[i],
            device_id=where, device_id_type=MESH,
        )
        @pl.when(receives if act == "recv" else sends)
        def _():
            if act == "start":
                copy.start()
            elif act == "recv":
                copy.wait_recv()
            else:
                copy.wait_send()

    for i in (2, 3, 4, 5):
        link(i, "start")
    for o in range(1, rows):
        forward_copy(0, o).start()
    for i in (0, 1):
        link(i, "start")
    got[0, pl.ds(my_row, R), :] = spec[:, pl.ds(my_col, L)]

    def columns_forward(kind, source):
        @pl.loop(0, R // 32)
        def _(i):
            strip = pl.ds(pl.multiple_of(i * 32, 32), 32)
            xh[strip, :], xl[strip, :] = halves(source[strip, :])

        @pl.loop(1, rows + 1)
        def _(o):
            at = pl.ds(pl.multiple_of(lax.rem(z + o, rows) * L, L), L)
            sent[kind - 1, :, at] = product(xh[...], xl[...], t_hi[:, at], t_lo[:, at])

            @pl.when(o < rows)
            def _():
                forward_copy(kind, o).start()

        got[kind, pl.ds(my_row, R), :] = sent[kind - 1, :, pl.ds(my_col, L)]

    columns_forward(1, obs)
    columns_forward(2, est)

    column = lax.broadcasted_iota(jnp.int32, (STRIP, N), 1)
    strip_row = lax.broadcasted_iota(jnp.int32, (STRIP, N), 0)
    plane_at = jnp.zeros((STRIP, N), jnp.int32) + p

    def column_slope(x):
        return jnp.where(column < N - 1, pltpu.roll(x, N - 1, 1) - x, 0.0)

    def weight(x, ahead, below, plane_ok, row_at):
        slope_p = jnp.where(plane_ok, ahead - x, 0.0)
        slope_r = jnp.where(jnp.logical_and(row_at >= 0, row_at < N - 1), below - x, 0.0)
        slope_c = column_slope(x)
        size = jnp.sqrt(slope_p * slope_p + slope_r * slope_r + slope_c * slope_c)
        return 1.0 / jnp.maximum(size, HUBER_EDGE)

    for i in range(6):
        link(i, "recv")

    @pl.loop(0, R // STRIP + 1)
    def _(i):
        t = pl.multiple_of(i * STRIP, STRIP)
        block = v[pl.ds(t, STRIP + 8), :]
        w[pl.ds(t, STRIP), :] = weight(
            block[:STRIP], pp[pl.ds(t, STRIP), :], block[1 : STRIP + 1],
            plane_at < planes - 1, my_row + t - 8 + strip_row,
        )

    @pl.loop(0, R // STRIP)
    def _(i):
        t = pl.multiple_of(i * STRIP, STRIP)
        block = pm[pl.ds(t + 8, STRIP + 8), :]
        w_pm[pl.ds(t, STRIP), :] = weight(
            block[:STRIP], est[pl.ds(t, STRIP), :], block[1 : STRIP + 1],
            plane_at > 0, my_row + t + strip_row,
        )

    def regular(x, x_pm, x_pp, shift, out):
        @pl.loop(0, R // STRIP)
        def _(i):
            t = pl.multiple_of(i * STRIP, STRIP)
            block = x[pl.ds(t, STRIP + 16), :]
            here = block[8 : 8 + STRIP]
            weights = w[pl.ds(t, STRIP + 8), :]
            w_here, w_up = weights[8:], weights[7 : 7 + STRIP]
            at = my_row + t + strip_row
            behind = x_pm[pl.ds(t + shift, STRIP), :]
            ahead = x_pp[pl.ds(t + shift, STRIP), :]
            in_r = jnp.where(at > 0, w_up * (here - block[7 : 7 + STRIP]), 0.0)
            out_r = jnp.where(at < N - 1, w_here * (block[9 : 9 + STRIP] - here), 0.0)
            in_p = jnp.where(plane_at > 0, w_pm[pl.ds(t, STRIP), :] * (here - behind), 0.0)
            out_p = jnp.where(plane_at < planes - 1, w_here * (ahead - here), 0.0)
            out_c = w_here * column_slope(here)
            in_c = pltpu.roll(out_c, 1, 1)
            out[pl.ds(t, STRIP), :] = SMOOTHING * (
                (in_p - out_p) + (in_r - out_r) + (in_c - out_c)
            )

    regular(v, pm, pp, 8, smooth)
    columns_forward(3, smooth)

    def arrived(kind):
        @pl.loop(1, rows)
        def _(o):
            forward_copy(kind, o).wait_recv()

    def split_columns(source):
        @pl.loop(0, N // 128)
        def _(i):
            strip = pl.ds(pl.multiple_of(i * 128, 128), 128)
            yh[strip, :], yl[strip, :] = halves(source[strip, :])

    def row_forward(kind, finish):
        split_columns(got.at[kind])

        @pl.loop(0, N // tile)
        def _(i):
            at = pl.ds(pl.multiple_of(i * tile, tile), tile)
            finish(at, product(c_hi[at, :], c_lo[at, :], yh[...], yl[...]))

    def row_inverse(kind, source):
        split_columns(source)

        @pl.loop(1, rows + 1)
        def _(o):
            at = pl.ds(pl.multiple_of(lax.rem(z + o, rows) * R, R), R)
            back_sent[kind, at, :] = product(t_hi[at, :], t_lo[at, :], yh[...], yl[...])

            @pl.when(o < rows)
            def _():
                back_copy(kind, o).start()

        back_got[kind, :, pl.ds(my_col, L)] = back_sent[kind, pl.ds(my_row, R), :]

    def column_inverse(kind, finish):
        @pl.loop(1, rows)
        def _(o):
            back_copy(kind, o).wait_recv()

        @pl.loop(0, R // 32)
        def _(i):
            strip = pl.ds(pl.multiple_of(i * 32, 32), 32)
            xh[strip, :], xl[strip, :] = halves(back_got[kind, strip, :])

        @pl.loop(0, N // tile)
        def _(i):
            at = pl.ds(pl.multiple_of(i * tile, tile), tile)
            finish(at, product(xh[...], xl[...], c_hi[:, at], c_lo[:, at]))

    def keep_seen(at, spectral):
        seen[at, :] = spectral

    def keep_blurred(at, spectral):
        gain = got[0, at, :]
        seen[at, :] = gain * (seen[at, :] - gain * spectral)

    def keep_filtered(at, spectral):
        gain = got[0, at, :]
        seen[at, :] = gain * gain * (seen[at, :] - spectral)

    arrived(0)
    arrived(1)
    row_forward(1, keep_seen)
    arrived(2)
    row_forward(2, keep_blurred)
    row_inverse(0, seen)
    arrived(3)
    row_forward(3, keep_filtered)
    row_inverse(1, seen)

    acc_rr[...] = jnp.zeros_like(acc_rr)
    acc_dot[...] = jnp.zeros_like(acc_dot)

    def keep_residual(at, x):
        x = x - smooth[:, at]
        d[pl.ds(8, R), at] = x
        d_out[:, at] = x
        acc_rr[...] += folded(x * x)

    def keep_image(at, x):
        x = x + image[:, at]
        image[:, at] = x
        acc_dot[...] += folded(x * d_out[:, at])

    column_inverse(0, keep_residual)
    for i in (8, 9, 6, 7):
        link(i, "start")
    for i in (6, 7, 8, 9):
        link(i, "recv")
    regular(d, d_pm, d_pp, 0, image)
    column_inverse(1, keep_image)

    rr, dot = jnp.sum(acc_rr[...]), jnp.sum(acc_dot[...])
    which = lax.broadcasted_iota(jnp.int32, (8, 128), 0)
    part[...] = jnp.where(which == 0, rr, dot)

    def row_sum(o):
        return pltpu.make_async_remote_copy(
            src_ref=part, dst_ref=red_rows.at[o - 1],
            send_sem=sum_send.at[o], recv_sem=sum_recv.at[o],
            device_id=(p, lax.rem(z + o, rows)), device_id_type=MESH,
        )

    def plane_sum(o):
        return pltpu.make_async_remote_copy(
            src_ref=total, dst_ref=red_planes.at[o - 1],
            send_sem=sum2_send.at[o], recv_sem=sum2_recv.at[o],
            device_id=(lax.rem(p + o, planes), z), device_id_type=MESH,
        )

    for o in range(1, rows):
        row_sum(o).start()
    value = part[...]
    for o in range(1, rows):
        row_sum(o).wait_recv()
        value = value + red_rows[o - 1]
    total[...] = value
    for o in range(1, planes):
        plane_sum(o).start()
    for o in range(1, planes):
        plane_sum(o).wait_recv()
        value = value + red_planes[o - 1]
    step_out[...] = jnp.broadcast_to(value[0:1] / value[1:2], (8, 128))

    @pl.loop(1, rows)
    def _(o):
        for kind in range(4):
            forward_copy(kind, o).wait_send()
        for kind in range(2):
            back_copy(kind, o).wait_send()
        row_sum(o).wait_send()

    for o in range(1, planes):
        plane_sum(o).wait_send()
    for i in range(10):
        link(i, "send")


def shards(observed, estimate, spectrum):
    R, N = observed.shape[1:]
    planes, rows = lax.axis_size("planes"), lax.axis_size("rows")
    assert observed.shape[0] == 1
    L = N // rows
    high, low = cosine_parts(N)
    tile = min(256, N)
    vmem = pl.BlockSpec(memory_space=pltpu.VMEM)
    field, padded = pltpu.VMEM((R, N), F32), pltpu.VMEM((R + 16, N), F32)
    tiles = lambda *lead: pltpu.VMEM(lead + (8, 128), F32)
    dma = lambda *shape: pltpu.SemaphoreType.DMA(shape)
    direction, image, step = pl.pallas_call(
        functools.partial(kernel, planes, rows),
        out_shape=(
            jax.ShapeDtypeStruct((R, N), F32),
            jax.ShapeDtypeStruct((R, N), F32),
            jax.ShapeDtypeStruct((8, 128), F32),
        ),
        in_specs=[vmem] * 7,
        out_specs=(vmem,) * 3,
        scratch_shapes=[
            padded, padded, padded, padded, field, field, padded, field, field,
            pltpu.VMEM((3, R, N), F32),
            pltpu.VMEM((4, N, L), F32),
            pltpu.VMEM((2, N, L), F32),
            pltpu.VMEM((2, R, N), F32),
            pltpu.VMEM((N, L), F32),
            pltpu.VMEM((R, N), BF16), pltpu.VMEM((R, N), BF16),
            pltpu.VMEM((N, L), BF16), pltpu.VMEM((N, L), BF16),
            pltpu.VMEM((8, tile), F32), pltpu.VMEM((8, tile), F32),
            tiles(), tiles(), tiles(rows - 1), tiles(planes - 1),
            dma(6, rows), dma(6, rows), dma(10), dma(10),
            dma(rows), dma(rows), dma(planes), dma(planes),
        ],
        compiler_params=pltpu.CompilerParams(
            collective_id=0, has_side_effects=True, vmem_limit_bytes=VMEM_LIMIT
        ),
        name="deconvolve",
    )(
        observed[0], estimate[0], spectrum[0],
        jnp.asarray(high), jnp.asarray(low),
        jnp.asarray(np.ascontiguousarray(high.T)), jnp.asarray(np.ascontiguousarray(low.T)),
    )
    step = step[0, 0]
    return (estimate + step * direction[None], (direction - step * image)[None])


def solution(mesh):
    return jax.shard_map(
        shards,
        mesh=mesh,
        in_specs=(P("planes", "rows", None), P("planes", "rows", None), P("planes", "rows", None)),
        out_specs=(P("planes", "rows", None), P("planes", "rows", None)),
        check_vma=False,
    )
```

profile of v0, /device:TPU:0, one launch (start us, length us, event | category | flops | bytes accessed | tf_op | source)
XLA Modules:
  0.0 184.4 jit_solution(10086109594717729484)
XLA Ops:
  0.6 177.2 %deconvolve.1 = (f32[256,1024]{1,0:T(8,128)}, f32[256,1024]{1,0:T(8,128)}, f32[8,128]{1,0:T(8,128)}) custom-call(f32[256,1024]{1,0:T(8,128)} %bitcast.9, f32[256,1024]{1,0:T(8,128)} %bitcast.8, f32[256,1024]{1,0:T(8,128)} %bitcast.10, bf16[1024,1024]{1,0:T(8,128)(2,1)} %constant.8.clone.c_hi, bf16[1024,1024]{1,0:T(8,128)(2,1)} %constant.9.clone.c_lo, ...), custom_call_target="tpu_custom_call" | custom-call | tf_op jit(solution)/shard_map/deconvolve/pallas_call | solution.py:381
  177.9 0.0 copy-start
  177.9 0.0 copy-start.1
  177.9 1.4 slice.3
  179.3 3.3 %subtract_bitcast_fusion = f32[1,256,1024]{2,1,0:T(8,128)} fusion(f32[256,1024]{1,0:T(8,128)} %get-tuple-element.6, f32[256,1024]{1,0:T(8,128)} %get-tuple-element.7, f32[]{:T(128)} %bitcast.3), kind=kLoop, calls=%fused_computation.1 | loop fusion | flops 524288 | bytes 3145732 | tf_op jit(solution)/shard_map/broadcast_in_dim | solution.py:414
  182.6 0.0 copy-done
  182.6 0.0 copy-done.1
  182.6 1.7 bitcast_add_fusion
Async XLA Ops:
  177.9 4.8 %copy-start = (f32[256,1024]{1,0:T(8,128)S(1)}, f32[256,1024]{1,0:T(8,128)}, u32[]{:S(2)}) copy-start(f32[256,1024]{1,0:T(8,128)} %get-tuple-element.6) | copy-start | bytes 3145732
  177.9 4.7 %copy-start.1 = (f32[1,256,1024]{2,1,0:T(8,128)S(1)}, f32[1,256,1024]{2,1,0:T(8,128)}, u32[]{:S(2)}) copy-start(f32[1,256,1024]{2,1,0:T(8,128)} %param.8) | copy-start | bytes 3145732
where the time goes:
time: 185 us; the launch traced here: 184 us
  Pallas kernels  177 us (96%)
  other arithmetic  5.09 us (3%)
    pallas_call x1, Pallas kernels, shards(): pl.pallas_call(functools.partial(kernel, planes, rows), out_shape=(jax.Sh...  177 us

commit v1 on v0

--- a/solution.py
+++ b/solution.py
@@ -46,7 +46,7 @@
 def kernel(
     planes, rows,
     obs, est, spec, c_hi, c_lo, t_hi, t_lo,
-    d_out, image, step_out,
+    restored, image,
     v, pp, pm, w, w_pm, smooth, d, d_pp, d_pm,
     sent, got, back_sent, back_got, seen, xh, xl, yh, yl,
     acc_rr, acc_dot, part, total, red_rows, red_planes,
@@ -101,19 +101,24 @@
             device_id_type=MESH,
         )
 
-    def back_copy(kind, o):
+    half = R // 2
+
+    def back_copy(kind, o, part_at=0):
         to = lax.rem(z + o, rows)
+        length = half if kind == 0 else R
+        start = pl.multiple_of(to * R + part_at * half, half)
         return pltpu.make_async_remote_copy(
-            src_ref=back_sent.at[kind, pl.ds(pl.multiple_of(to * R, R), R), :],
-            dst_ref=back_got.at[kind, :, pl.ds(my_col, L)],
-            send_sem=send_sem.at[kind + 4, o],
-            recv_sem=recv_sem.at[kind + 4, o],
+            src_ref=back_sent.at[kind, pl.ds(start, length), :],
+            dst_ref=back_got.at[kind, pl.ds(part_at * half, length), pl.ds(my_col, L)],
+            send_sem=send_sem.at[4 + 2 * kind + part_at, o],
+            recv_sem=recv_sem.at[4 + 2 * kind + part_at, o],
             device_id=(p, to),
             device_id_type=MESH,
         )
 
     first, last = pl.ds(0, 8), pl.ds(R - 8, 8)
     body = pl.ds(8, R)
+    top, low = pl.ds(8, half), pl.ds(8 + half, half)
     both = jnp.logical_and
     links = [
         (est, pm.at[body, :], (p + 1, z), has_pp, has_pm),
@@ -122,10 +127,12 @@
         (est.at[first, :], v.at[pl.ds(R + 8, 8), :], (p, z - 1), has_up, has_dn),
         (est.at[last, :], pp.at[pl.ds(0, 8), :], (p - 1, z + 1), both(has_pm, has_dn), both(has_pp, has_up)),
         (est.at[first, :], pm.at[pl.ds(R + 8, 8), :], (p + 1, z - 1), both(has_pp, has_up), both(has_pm, has_dn)),
-        (d.at[body, :], d_pm, (p + 1, z), has_pp, has_pm),
-        (d.at[body, :], d_pp, (p - 1, z), has_pm, has_pp),
+        (d.at[top, :], d_pm.at[pl.ds(0, half), :], (p + 1, z), has_pp, has_pm),
+        (d.at[top, :], d_pp.at[pl.ds(0, half), :], (p - 1, z), has_pm, has_pp),
         (d.at[pl.ds(R, 8), :], d.at[pl.ds(0, 8), :], (p, z + 1), has_dn, has_up),
         (d.at[pl.ds(8, 8), :], d.at[pl.ds(R + 8, 8), :], (p, z - 1), has_up, has_dn),
+        (d.at[low, :], d_pm.at[pl.ds(half, half), :], (p + 1, z), has_pp, has_pm),
+        (d.at[low, :], d_pp.at[pl.ds(half, half), :], (p - 1, z), has_pm, has_pp),
     ]
 
     def link(i, act):
@@ -162,9 +169,10 @@
             at = pl.ds(pl.multiple_of(lax.rem(z + o, rows) * L, L), L)
             sent[kind - 1, :, at] = product(xh[...], xl[...], t_hi[:, at], t_lo[:, at])
 
-            @pl.when(o < rows)
-            def _():
-                forward_copy(kind, o).start()
+            if kind != 3:
+                @pl.when(o < rows)
+                def _():
+                    forward_copy(kind, o).start()
 
         got[kind, pl.ds(my_row, R), :] = sent[kind - 1, :, pl.ds(my_col, L)]
 
@@ -206,8 +214,8 @@
             plane_at > 0, my_row + t + strip_row,
         )
 
-    def regular(x, x_pm, x_pp, shift, out):
-        @pl.loop(0, R // STRIP)
+    def regular(x, x_pm, x_pp, shift, out, begin=0, end=R):
+        @pl.loop(begin // STRIP, end // STRIP)
         def _(i):
             t = pl.multiple_of(i * STRIP, STRIP)
             block = x[pl.ds(t, STRIP + 16), :]
@@ -230,6 +238,11 @@
     regular(v, pm, pp, 8, smooth)
     columns_forward(3, smooth)
 
+    @pl.loop(1, rows)
+    def _(o):
+        forward_copy(2, o).wait_send()
+        forward_copy(3, o).start()
+
     def arrived(kind):
         @pl.loop(1, rows)
         def _(o):
@@ -251,32 +264,38 @@
 
     def row_inverse(kind, source):
         split_columns(source)
-
-        @pl.loop(1, rows + 1)
-        def _(o):
-            at = pl.ds(pl.multiple_of(lax.rem(z + o, rows) * R, R), R)
-            back_sent[kind, at, :] = product(t_hi[at, :], t_lo[at, :], yh[...], yl[...])
-
-            @pl.when(o < rows)
-            def _():
-                back_copy(kind, o).start()
+        length = half if kind == 0 else R
+        for part_at in range(R // length):
+            @pl.loop(1, rows + 1)
+            def _(o):
+                to = lax.rem(z + o, rows)
+                at = pl.ds(pl.multiple_of(to * R + part_at * half, half), length)
+                back_sent[kind, at, :] = product(t_hi[at, :], t_lo[at, :], yh[...], yl[...])
+
+                if kind == 0:
+                    @pl.when(o < rows)
+                    def _():
+                        back_copy(kind, o, part_at).start()
 
         back_got[kind, :, pl.ds(my_col, L)] = back_sent[kind, pl.ds(my_row, R), :]
 
-    def column_inverse(kind, finish):
+    def column_inverse(kind, part_at, finish):
         @pl.loop(1, rows)
         def _(o):
-            back_copy(kind, o).wait_recv()
-
-        @pl.loop(0, R // 32)
-        def _(i):
-            strip = pl.ds(pl.multiple_of(i * 32, 32), 32)
+            back_copy(kind, o, part_at).wait_recv()
+
+        length = half if kind == 0 else R
+        here = pl.ds(part_at * half, length)
+
+        @pl.loop(0, length // 16)
+        def _(i):
+            strip = pl.ds(pl.multiple_of(part_at * half + i * 16, 16), 16)
             xh[strip, :], xl[strip, :] = halves(back_got[kind, strip, :])
 
         @pl.loop(0, N // tile)
         def _(i):
             at = pl.ds(pl.multiple_of(i * tile, tile), tile)
-            finish(at, product(xh[...], xl[...], c_hi[:, at], c_lo[:, at]))
+            finish(at, product(xh[here, :], xl[here, :], c_hi[:, at], c_lo[:, at]))
 
     def keep_seen(at, spectral):
         seen[at, :] = spectral
@@ -302,24 +321,37 @@
     acc_rr[...] = jnp.zeros_like(acc_rr)
     acc_dot[...] = jnp.zeros_like(acc_dot)
 
-    def keep_residual(at, x):
-        x = x - smooth[:, at]
-        d[pl.ds(8, R), at] = x
-        d_out[:, at] = x
+    def keep_residual(part_at, at, x):
+        here = pl.ds(part_at * half, half)
+        x = x - smooth[here, at]
+        d[pl.ds(8 + part_at * half, half), at] = x
         acc_rr[...] += folded(x * x)
 
     def keep_image(at, x):
         x = x + image[:, at]
         image[:, at] = x
-        acc_dot[...] += folded(x * d_out[:, at])
-
-    column_inverse(0, keep_residual)
-    for i in (8, 9, 6, 7):
+        acc_dot[...] += folded(x * d[pl.ds(8, R), at])
+
+    column_inverse(0, 0, functools.partial(keep_residual, 0))
+    for i in (9, 6, 7):
         link(i, "start")
-    for i in (6, 7, 8, 9):
+
+    @pl.loop(1, rows)
+    def _(o):
+        back_copy(0, o, 0).wait_send()
+        back_copy(0, o, 1).wait_send()
+        back_copy(1, o).start()
+
+    column_inverse(0, 1, functools.partial(keep_residual, 1))
+    for i in (8, 10, 11):
+        link(i, "start")
+    for i in (6, 7, 8):
         link(i, "recv")
-    regular(d, d_pm, d_pp, 0, image)
-    column_inverse(1, keep_image)
+    regular(d, d_pm, d_pp, 0, image, 0, half)
+    for i in (9, 10, 11):
+        link(i, "recv")
+    regular(d, d_pm, d_pp, 0, image, half, R)
+    column_inverse(1, 0, keep_image)
 
     rr, dot = jnp.sum(acc_rr[...]), jnp.sum(acc_dot[...])
     which = lax.broadcasted_iota(jnp.int32, (8, 128), 0)
@@ -351,19 +383,26 @@
     for o in range(1, planes):
         plane_sum(o).wait_recv()
         value = value + red_planes[o - 1]
-    step_out[...] = jnp.broadcast_to(value[0:1] / value[1:2], (8, 128))
+    total_step = value[0:1, 0:1] / value[1:2, 0:1]
+
+    @pl.loop(0, R // STRIP)
+    def _(i):
+        t = pl.multiple_of(i * STRIP, STRIP)
+        strip = pl.ds(t, STRIP)
+        here = d[pl.ds(t + 8, STRIP), :]
+        restored[strip, :] = est[strip, :] + total_step * here
+        image[strip, :] = here - total_step * image[strip, :]
 
     @pl.loop(1, rows)
     def _(o):
-        for kind in range(4):
+        for kind in (0, 1, 3):
             forward_copy(kind, o).wait_send()
-        for kind in range(2):
-            back_copy(kind, o).wait_send()
+        back_copy(1, o).wait_send()
         row_sum(o).wait_send()
 
     for o in range(1, planes):
         plane_sum(o).wait_send()
-    for i in range(10):
+    for i in range(12):
         link(i, "send")
 
 
@@ -378,15 +417,14 @@
     field, padded = pltpu.VMEM((R, N), F32), pltpu.VMEM((R + 16, N), F32)
     tiles = lambda *lead: pltpu.VMEM(lead + (8, 128), F32)
     dma = lambda *shape: pltpu.SemaphoreType.DMA(shape)
-    direction, image, step = pl.pallas_call(
+    restored, residual = pl.pallas_call(
         functools.partial(kernel, planes, rows),
         out_shape=(
             jax.ShapeDtypeStruct((R, N), F32),
             jax.ShapeDtypeStruct((R, N), F32),
-            jax.ShapeDtypeStruct((8, 128), F32),
         ),
         in_specs=[vmem] * 7,
-        out_specs=(vmem,) * 3,
+        out_specs=(vmem,) * 2,
         scratch_shapes=[
             padded, padded, padded, padded, field, field, padded, field, field,
             pltpu.VMEM((3, R, N), F32),
@@ -398,7 +436,7 @@
             pltpu.VMEM((N, L), BF16), pltpu.VMEM((N, L), BF16),
             pltpu.VMEM((8, tile), F32), pltpu.VMEM((8, tile), F32),
             tiles(), tiles(), tiles(rows - 1), tiles(planes - 1),
-            dma(6, rows), dma(6, rows), dma(10), dma(10),
+            dma(7, rows), dma(7, rows), dma(12), dma(12),
             dma(rows), dma(rows), dma(planes), dma(planes),
         ],
         compiler_params=pltpu.CompilerParams(
@@ -410,8 +448,7 @@
         jnp.asarray(high), jnp.asarray(low),
         jnp.asarray(np.ascontiguousarray(high.T)), jnp.asarray(np.ascontiguousarray(low.T)),
     )
-    step = step[0, 0]
-    return (estimate + step * direction[None], (direction - step * image)[None])
+    return (restored[None], residual[None])
 
 
 def solution(mesh):

time: 185 us -> 170 us (0.919)
  Pallas kernels: 177 us -> 166 us
  other arithmetic: 5.09 us -> 0 us
  local copies, waits for them, and re-layouts: 1.39 us -> 3.37 us
    pallas_call x1, Pallas kernels: 177 us -> 166 us  [shards(): pl.pallas_call(functools.partial(kernel, planes, rows), out_shape=(jax.Sh...]
    unnamed x4, local copies, waits for them, and re-layouts: 0.01 us -> 3.37 us
    broadcast_in_dim x1 -> x0, other arithmetic: 3.35 us -> none  [shards(): return (estimate + step * direction[None], (direction - step * image)[None])]
where the time goes in v1:
time: 170 us
  Pallas kernels  166 us (98%)
  local copies, waits for them, and re-layouts  3.37 us (2%)
    pallas_call x1, Pallas kernels, shards(): pl.pallas_call(functools.partial(kernel, planes, rows), out_shape=(jax.Sh...  166 us

profile of v1, /device:TPU:0, one launch (start us, length us, event | category | flops | bytes accessed | tf_op | source)
XLA Modules:
  0.0 170.0 jit_solution(8816910877497992550)
XLA Ops:
  0.6 165.9 %deconvolve.1 = (f32[256,1024]{1,0:T(8,128)}, f32[256,1024]{1,0:T(8,128)}) custom-call(f32[256,1024]{1,0:T(8,128)} %bitcast.7, f32[256,1024]{1,0:T(8,128)} %bitcast.8, f32[256,1024]{1,0:T(8,128)} %bitcast.9, bf16[1024,1024]{1,0:T(8,128)(2,1)} %constant.8.clone.c_hi, bf16[1024,1024]{1,0:T(8,128)(2,1)} %constant.9.clone.c_lo, ...), custom_call_target="tpu_custom_call" | custom-call | tf_op jit(solution)/shard_map/deconvolve/pallas_call | solution.py:420
  166.6 0.0 copy-start
  166.6 2.4 %copy.11 = f32[1,256,1024]{2,1,0:T(8,128)} copy(f32[1,256,1024]{2,1,0:T(8,128)} %bitcast.6) | data formatting | bytes 2097152
  169.0 0.0 copy-done
  169.0 1.0 copy.12
Async XLA Ops:
  166.6 2.4 %copy-start = (f32[256,1024]{1,0:T(8,128)S(1)}, f32[256,1024]{1,0:T(8,128)}, u32[]{:S(2)}) copy-start(f32[256,1024]{1,0:T(8,128)} %get-tuple-element.5) | copy-start | bytes 3145732

commit v2 on v1

--- a/solution.py
+++ b/solution.py
@@ -45,10 +45,11 @@
 
 def kernel(
     planes, rows,
-    obs, est, spec, c_hi, c_lo, t_hi, t_lo,
+    obs, est, spec, c_hi_far, c_lo_far, t_hi_far, t_lo_far,
     restored, image,
     v, pp, pm, w, w_pm, smooth, d, d_pp, d_pm,
     sent, got, back_sent, back_got, seen, xh, xl, yh, yl,
+    c_hi, c_lo, t_hi, t_lo, table_sem,
     acc_rr, acc_dot, part, total, red_rows, red_planes,
     send_sem, recv_sem, halo_send, halo_recv, sum_send, sum_recv, sum2_send, sum2_recv,
 ):
@@ -61,6 +62,14 @@
     has_pm, has_pp = p > 0, p < planes - 1
     has_up, has_dn = z > 0, z < rows - 1
 
+    tables = [
+        pltpu.make_async_copy(far, near, table_sem.at[i])
+        for i, (far, near) in enumerate(
+            ((t_hi_far, t_hi), (t_lo_far, t_lo), (c_hi_far, c_hi), (c_lo_far, c_lo))
+        )
+    ]
+    for table in tables:
+        table.start()
     v[pl.ds(8, R), :] = est[...]
 
     barrier = pltpu.get_barrier_semaphore()
@@ -103,9 +112,9 @@
 
     half = R // 2
 
-    def back_copy(kind, o, part_at=0):
+    def back_copy(kind, o, part_at):
         to = lax.rem(z + o, rows)
-        length = half if kind == 0 else R
+        length = half
         start = pl.multiple_of(to * R + part_at * half, half)
         return pltpu.make_async_remote_copy(
             src_ref=back_sent.at[kind, pl.ds(start, length), :],
@@ -176,6 +185,8 @@
 
         got[kind, pl.ds(my_row, R), :] = sent[kind - 1, :, pl.ds(my_col, L)]
 
+    for table in tables[:2]:
+        table.wait()
     columns_forward(1, obs)
     columns_forward(2, est)
 
@@ -214,7 +225,7 @@
             plane_at > 0, my_row + t + strip_row,
         )
 
-    def regular(x, x_pm, x_pp, shift, out, begin=0, end=R):
+    def regular(x, x_pm, x_pp, shift, out, begin=0, end=R, add=False):
         @pl.loop(begin // STRIP, end // STRIP)
         def _(i):
             t = pl.multiple_of(i * STRIP, STRIP)
@@ -231,9 +242,10 @@
             out_p = jnp.where(plane_at < planes - 1, w_here * (ahead - here), 0.0)
             out_c = w_here * column_slope(here)
             in_c = pltpu.roll(out_c, 1, 1)
-            out[pl.ds(t, STRIP), :] = SMOOTHING * (
-                (in_p - out_p) + (in_r - out_r) + (in_c - out_c)
-            )
+            result = SMOOTHING * ((in_p - out_p) + (in_r - out_r) + (in_c - out_c))
+            out[pl.ds(t, STRIP), :] = result
+            if add:
+                acc_dot[...] += folded(result * here)
 
     regular(v, pm, pp, 8, smooth)
     columns_forward(3, smooth)
@@ -264,8 +276,8 @@
 
     def row_inverse(kind, source):
         split_columns(source)
-        length = half if kind == 0 else R
-        for part_at in range(R // length):
+        length = half
+        for part_at in range(2):
             @pl.loop(1, rows + 1)
             def _(o):
                 to = lax.rem(z + o, rows)
@@ -284,7 +296,7 @@
         def _(o):
             back_copy(kind, o, part_at).wait_recv()
 
-        length = half if kind == 0 else R
+        length = half
         here = pl.ds(part_at * half, length)
 
         @pl.loop(0, length // 16)
@@ -306,8 +318,14 @@
 
     def keep_filtered(at, spectral):
         gain = got[0, at, :]
-        seen[at, :] = gain * gain * (seen[at, :] - spectral)
-
+        moved = gain * (seen[at, :] - spectral)
+        acc_dot[:, pl.ds(0, L)] += folded(moved * moved)
+        seen[at, :] = gain * moved
+
+    for table in tables[2:]:
+        table.wait()
+    acc_rr[...] = jnp.zeros_like(acc_rr)
+    acc_dot[...] = jnp.zeros_like(acc_dot)
     arrived(0)
     arrived(1)
     row_forward(1, keep_seen)
@@ -318,20 +336,12 @@
     row_forward(3, keep_filtered)
     row_inverse(1, seen)
 
-    acc_rr[...] = jnp.zeros_like(acc_rr)
-    acc_dot[...] = jnp.zeros_like(acc_dot)
-
     def keep_residual(part_at, at, x):
         here = pl.ds(part_at * half, half)
         x = x - smooth[here, at]
         d[pl.ds(8 + part_at * half, half), at] = x
         acc_rr[...] += folded(x * x)
 
-    def keep_image(at, x):
-        x = x + image[:, at]
-        image[:, at] = x
-        acc_dot[...] += folded(x * d[pl.ds(8, R), at])
-
     column_inverse(0, 0, functools.partial(keep_residual, 0))
     for i in (9, 6, 7):
         link(i, "start")
@@ -340,18 +350,23 @@
     def _(o):
         back_copy(0, o, 0).wait_send()
         back_copy(0, o, 1).wait_send()
-        back_copy(1, o).start()
+        back_copy(1, o, 0).start()
 
     column_inverse(0, 1, functools.partial(keep_residual, 1))
     for i in (8, 10, 11):
         link(i, "start")
+
+    @pl.loop(1, rows)
+    def _(o):
+        back_copy(1, o, 0).wait_send()
+        back_copy(1, o, 1).start()
+
     for i in (6, 7, 8):
         link(i, "recv")
-    regular(d, d_pm, d_pp, 0, image, 0, half)
+    regular(d, d_pm, d_pp, 0, image, 0, half, True)
     for i in (9, 10, 11):
         link(i, "recv")
-    regular(d, d_pm, d_pp, 0, image, half, R)
-    column_inverse(1, 0, keep_image)
+    regular(d, d_pm, d_pp, 0, image, half, R, True)
 
     rr, dot = jnp.sum(acc_rr[...]), jnp.sum(acc_dot[...])
     which = lax.broadcasted_iota(jnp.int32, (8, 128), 0)
@@ -393,11 +408,18 @@
         restored[strip, :] = est[strip, :] + total_step * here
         image[strip, :] = here - total_step * image[strip, :]
 
+    def keep_updated(part_at, at, x):
+        here = pl.ds(part_at * half, half)
+        image[here, at] = image[here, at] - total_step * x
+
+    column_inverse(1, 0, functools.partial(keep_updated, 0))
+    column_inverse(1, 1, functools.partial(keep_updated, 1))
+
     @pl.loop(1, rows)
     def _(o):
         for kind in (0, 1, 3):
             forward_copy(kind, o).wait_send()
-        back_copy(1, o).wait_send()
+        back_copy(1, o, 1).wait_send()
         row_sum(o).wait_send()
 
     for o in range(1, planes):
@@ -423,7 +445,7 @@
             jax.ShapeDtypeStruct((R, N), F32),
             jax.ShapeDtypeStruct((R, N), F32),
         ),
-        in_specs=[vmem] * 7,
+        in_specs=[vmem] * 3 + [pl.BlockSpec(memory_space=pl.ANY)] * 4,
         out_specs=(vmem,) * 2,
         scratch_shapes=[
             padded, padded, padded, padded, field, field, padded, field, field,
@@ -434,9 +456,10 @@
             pltpu.VMEM((N, L), F32),
             pltpu.VMEM((R, N), BF16), pltpu.VMEM((R, N), BF16),
             pltpu.VMEM((N, L), BF16), pltpu.VMEM((N, L), BF16),
-            pltpu.VMEM((8, tile), F32), pltpu.VMEM((8, tile), F32),
+            *[pltpu.VMEM((N, N), BF16)] * 4, dma(4),
+            pltpu.VMEM((8, tile), F32), pltpu.VMEM((8, N), F32),
             tiles(), tiles(), tiles(rows - 1), tiles(planes - 1),
-            dma(7, rows), dma(7, rows), dma(12), dma(12),
+            dma(8, rows), dma(8, rows), dma(12), dma(12),
             dma(rows), dma(rows), dma(planes), dma(planes),
         ],
         compiler_params=pltpu.CompilerParams(

time: 170 us -> 164 us (0.965)
  Pallas kernels: 166 us -> 160 us
    pallas_call x1, Pallas kernels: 166 us -> 160 us  [shards(): pl.pallas_call(functools.partial(kernel, planes, rows), out_shape=(jax.Sh...]
where the time goes in v2:
time: 164 us
  Pallas kernels  160 us (98%)
  local copies, waits for them, and re-layouts  3.37 us (2%)
    pallas_call x1, Pallas kernels, shards(): pl.pallas_call(functools.partial(kernel, planes, rows), out_shape=(jax.Sh...  160 us
    unnamed x4, local copies, waits for them, and re-layouts  3.37 us

profile of v2, /device:TPU:0, one launch (start us, length us, event | category | flops | bytes accessed | tf_op | source)
XLA Modules:
  0.0 164.0 jit_solution(8730515043242870893)
XLA Ops:
  0.6 160.0 %deconvolve.1 = (f32[256,1024]{1,0:T(8,128)}, f32[256,1024]{1,0:T(8,128)}) custom-call(f32[256,1024]{1,0:T(8,128)} %bitcast.7, f32[256,1024]{1,0:T(8,128)} %bitcast.8, f32[256,1024]{1,0:T(8,128)} %bitcast.9, bf16[1024,1024]{1,0:T(8,128)(2,1)} %constant.8.clone.c_hi_far, bf16[1024,1024]{1,0:T(8,128)(2,1)} %constant.9.clone.c_lo_far, ...), custom_call_target="tpu_custom_call" | custom-call | tf_op jit(solution)/shard_map/deconvolve/pallas_call | solution.py:442
  160.7 0.0 copy-start
  160.7 2.4 %copy.11 = f32[1,256,1024]{2,1,0:T(8,128)} copy(f32[1,256,1024]{2,1,0:T(8,128)} %bitcast.6) | data formatting | bytes 2097152
  163.1 0.0 copy-done
  163.1 1.0 copy.12
Async XLA Ops:
  160.7 2.4 %copy-start = (f32[256,1024]{1,0:T(8,128)S(1)}, f32[256,1024]{1,0:T(8,128)}, u32[]{:S(2)}) copy-start(f32[256,1024]{1,0:T(8,128)} %get-tuple-element.5) | copy-start | bytes 3145732
